TPU v7x, 512 devices: a whole 4x4x16 slice. The times are simulated.
512 devices in a mesh: section: 8 (over y, core), row: 4 (over x), col: 16 (over z).
Axes of the slice: x: 4, y: 4, z: 16, core: 2. Of those that a mesh axis runs over, the one named last changes fastest.
Arguments:
- weights: bfloat16 [8192, 106496], P('row', ('section', 'col')), may hold values from -12 to 12
- sketch: bfloat16 [106496, 256], P(('section', 'col')), may hold values from -100 to 100
Outputs:
- shared_basis: bfloat16 [8192, 256], P('row')
- coefficients: float32 [256, 106496], P('row', ('section', 'col'))
All inputs are finite; a program needn't handle non-finite values.
Results may differ from a plain program's by a relative error of at most 0.0027.
Values may be sent and summed in bfloat16 or wider, within the bound.
A program may use at most 64 MiB of HBM per device.

v0:
```python
import math

import jax
import jax.numpy as jnp
from jax import lax
from jax.sharding import PartitionSpec as P

D = 8192


def gram_from(sample_rows):
    return lax.dot_general(
        sample_rows,
        sample_rows,
        (((0,), (0,)), ((), ())),
        precision=lax.Precision.HIGHEST,
        preferred_element_type=jnp.float32,
    )


def invert_lower(gram_matrix):
    lower_factor = jnp.linalg.cholesky(gram_matrix)
    identity = jnp.eye(gram_matrix.shape[0], dtype=jnp.float32)
    return jax.scipy.linalg.solve_triangular(lower_factor, identity, lower=True)


def to_basis(sample_rows, inverse_factor):
    product = jnp.dot(sample_rows, inverse_factor.T, precision=lax.Precision.HIGHEST)
    return (math.sqrt(D) * product).astype(jnp.bfloat16)


def shards(weights, sketch):
    local_sample = jnp.dot(weights, sketch, preferred_element_type=jnp.float32)
    sample = lax.psum(local_sample, ("section", "col"))
    gram_matrix = lax.psum(gram_from(sample), "row")
    shared_basis = to_basis(sample, invert_lower(gram_matrix))
    product = lax.dot_general(
        shared_basis, weights, (((0,), (0,)), ((), ())), preferred_element_type=jnp.float32
    )
    coefficients = lax.psum_scatter(product / math.sqrt(D), "row", scatter_dimension=0, tiled=True)
    return (shared_basis, coefficients)


def solution(mesh):
    placed = (P("row", ("section", "col")), P(("section", "col"), None))
    return jax.shard_map(
        shards,
        mesh=mesh,
        in_specs=placed,
        out_specs=(P("row", None), P("row", ("section", "col"))),
        check_vma=False,
    )
```

profile of v0, /device:TPU:1, one launch (start us, length us, event | category | flops | bytes accessed | tf_op | source)
XLA Modules:
  0.0 551.7 jit_solution(10950016737213920827)
XLA Ops:
  7.2 1.9 copy-done
  9.1 3.6 fusion.14
  12.8 353.1 %all-reduce.4.cloned.1.call-done = f32[2048,256]{1,0:T(8,128)} async-done(((f32[2048,256]{1,0:T(8,128)}), f32[2048,256]{1,0:T(8,128)}) %all-reduce.4.cloned.1.call-update) | async-done | bytes 2097168 | tf_op jit(solution)/shard_map/psum | solution.py:34
  365.9 6.4 %fusion.15 = f32[256,256]{0,1:T(8,128)} fusion(f32[2048,256]{1,0:T(8,128)} %all-reduce.4.cloned.1.call-done), kind=kOutput, calls=%fused_computation.37 | convolution fusion | flops 1610612736 | bytes 2359296 | tf_op jit(solution)/shard_map/dot_general | solution.py:12
  372.6 52.8 %all-reduce.6.cloned.1.call-done = f32[256,256]{0,1:T(8,128)} async-done(((f32[256,256]{0,1:T(8,128)}), f32[256,256]{0,1:T(8,128)}) %all-reduce.6.cloned.1.call-update) | async-done | bytes 262160 | tf_op jit(solution)/shard_map/psum | solution.py:35
  425.4 1.8 copy.5
  427.2 1.1 fusion.4
  429.6 12.5 %cholesky.50 = f32[128,128]{1,0:T(8,128)S(1)} custom-call(f32[128,128]{1,0:T(8,128)} %cholesky.118), custom_call_target="Cholesky" | custom-call | tf_op jit(solution)/shard_map/jit(cholesky)/cholesky | solution.py:22
  442.8 11.3 %custom-call.15 = f32[1,128,128]{1,2,0:T(8,128)} custom-call(f32[1,128,128]{2,1,0:T(8,128)} %get-tuple-element.23), custom_call_target="InvertDiagBlocksLowerTriangular" | custom-call | tf_op jit(solution)/shard_map/jit(cholesky)/cholesky | solution.py:22
  454.8 1.7 constant_dynamic-update-slice_fusion.1
  456.5 1.7 convolution_subtract_fusion.1
  458.2 12.5 %cholesky.105 = f32[128,128]{1,0:T(8,128)S(1)} custom-call(f32[128,128]{1,0:T(8,128)} %convolution_subtract_fusion.1), custom_call_target="Cholesky" | custom-call | tf_op jit(solution)/shard_map/jit(cholesky)/cholesky | solution.py:22
  473.3 1.7 select_select_fusion
  475.1 6.8 %while.1 = (s32[]{:T(128)}, f32[256,256]{1,0:T(8,128)}, s32[2,2]{1,0:T(2,128)S(1)}, f32[2,128,128]{2,1,0:T(8,128)}, s32[]{:T(128)}) while((s32[]{:T(128)}, f32[256,256]{1,0:T(8,128)}, s32[2,2]{1,0:T(2,128)S(1)}, f32[2,128,128]{2,1,0:T(8,128)}, s32[]{:T(128)}) %tuple.27), condition=%wide.while_cond, body=%wide.while_body.sunk | while | flops 2 | bytes 132705 | solution.py:24
  475.7 2.9 bitcast_dynamic-update-slice_fusion.2
  479.1 2.8 bitcast_dynamic-update-slice_fusion.2
  481.9 21.1 %custom-call.16 = f32[2,128,128]{1,2,0:T(8,128)} custom-call(f32[2,128,128]{2,1,0:T(8,128)} %get-tuple-element.9), custom_call_target="InvertDiagBlocksLowerTriangular" | custom-call | tf_op jit(solution)/shard_map/jit(_solve_triangular)/triangular_solve | solution.py:24
  503.0 1.1 fusion.5
  504.1 1.1 convolution_subtract_fusion
  505.2 1.1 fusion.8
  506.4 3.4 fusion
  509.8 1.0 copy-done.1
  510.8 2.3 convolution_multiply_fusion.1
  513.1 32.1 %reduce-scatter.2.cloned.1.call-done = f32[64,832]{1,0:T(8,128)} async-done(((f32[256,832]{1,0:T(8,128)}), f32[64,832]{1,0:T(8,128)}) %reduce-scatter.2.cloned.1.call-update) | async-done | bytes 213008 | tf_op jit(solution)/shard_map/reduce_scatter | solution.py:40
  (23 shorter events, 5.7 us)
Async XLA Ops:
  7.2 2.0 copy-start
  7.2 358.7 %all-reduce.4.cloned.1.call-start = ((), (), s32[]{:S(2)}) async-start(), calls=%async_computation.1 | async-start | bytes 4194304 | tf_op jit(solution)/shard_map/psum | solution.py:34
  12.8 412.6 %all-reduce.6.cloned.1.call-start = ((), (), s32[]{:S(2)}) async-start(), calls=%async_computation.2 | async-start | bytes 524288 | tf_op jit(solution)/shard_map/psum | solution.py:35
  372.3 172.8 %reduce-scatter.2.cloned.1.call-start = ((), (), s32[]{:S(2)}) async-start(), calls=%async_computation.3 | async-start | bytes 1146880 | tf_op jit(solution)/shard_map/reduce_scatter | solution.py:40
  428.2 0.7 copy-start.2
  509.8 1.0 copy-start.1
Sparse Core Ops, SparseCore 0:
  12.9 352.9 all-reduce.3
  372.4 52.8 all-reduce.5
  513.2 31.8 reduce-scatter.1
where the time goes:
time: 553 us; the launch traced here: 552 us
  waiting for transfers between devices  438 us (79%)
  other arithmetic  62.2 us (11%)
  matrix products  22.5 us (4%)
  between operations  15.1 us (3%)
  local copies, waits for them, and re-layouts  13.6 us (2%)
    psum x1, waiting for transfers between devices, shards(): sample = lax.psum(local_sample, ('section', 'col'))  353 us
    psum x1, waiting for transfers between devices, shards(): gram_matrix = lax.psum(gram_from(sample), 'row')  52.8 us
    another operation x6, other arithmetic, invert_lower(): lower_factor = jnp.linalg.cholesky(gram_matrix)  38.3 us
    reduce_scatter x1, waiting for transfers between devices, shards(): lax.psum_scatter(product / math.sqrt(D), 'row', scatter_dimension=0, tile...  32.1 us
    another operation x3, other arithmetic, invert_lower(): return jax.scipy.linalg.solve_triangular(lower_factor, identity, lower=True)  22.8 us
  transfers between devices with their start and end apart: 3, of which 3 were waited for; matrix products, arithmetic and copies ran while one was open for 0% of the time, Pallas kernels for 0%

commit v1 on v0

v1 whole, which is shorter than its diff:
```python
import functools
import math

import jax
import jax.numpy as jnp
from jax import lax
from jax.experimental import pallas as pl
from jax.experimental.pallas import tpu as pltpu
from jax.sharding import PartitionSpec as P

D = 8192
R = 256
MESH = pl.DeviceIdType.MESH


def sum_and_gram(w_hbm, s_ref, hi_out, lo_out, gram_out, w_ref, part, core_in, core_sum, y_in, y_sum, z_in, mine,
                 high, low, gram_part, gram_in, gram_all,
                 w_sem, core_ss, core_rs, y_ss, y_rs, z_ss, z_rs, hz_ss, hz_rs, hy_ss, hy_rs, hc_ss, hc_rs,
                 g_ss, g_rs, b_ss, b_rs, out_sem):
    section = lax.axis_index("section")
    row = lax.axis_index("row")
    col = lax.axis_index("col")
    core = lax.rem(section, 2)
    y = section // 2
    other = 1 - core
    sibling = {"section": 2 * y + other}

    def y_of(k):
        return lax.rem(y + k, 4)

    def z_of(k):
        return lax.rem(col + k, 16)

    def to_y(k):
        return {"section": 2 * y_of(k) + core}

    def to_z(k):
        return {"col": z_of(k)}

    def group_of(k):
        return lax.rem(row + k // 8, 4), lax.rem(section + k % 8, 8)

    def to_group(k):
        r, s = group_of(k)
        return {"row": r, "section": s}

    def send(src, dst, ss, rs, device):
        copy = pltpu.make_async_remote_copy(
            src_ref=src, dst_ref=dst, send_sem=ss, recv_sem=rs, device_id=device, device_id_type=MESH)
        copy.start()
        return copy

    loads = []
    for half in range(2):
        first = jnp.where(half == 0, other, core) * 1024
        load = pltpu.make_async_copy(
            w_hbm.at[pl.ds(pl.multiple_of(first, 1024), 1024)], w_ref.at[half], w_sem.at[half])
        load.start()
        loads.append(load)

    barrier = pltpu.get_barrier_semaphore()
    for k in range(1, 32):
        pl.semaphore_signal(barrier, inc=1, device_id=to_group(k), device_id_type=MESH)
    for k in range(1, 16):
        pl.semaphore_signal(barrier, inc=1, device_id=to_z(k), device_id_type=MESH)

    sent = []
    for half in range(2):
        loads[half].wait()

        @pl.loop(0, 4)
        def _(q):
            rows = pl.ds(pl.multiple_of(q * 256, 256), 256)
            product = jnp.dot(w_ref[half, rows, :], s_ref[...], preferred_element_type=jnp.float32)
            part[half, q] = product.reshape(16, 2, 8, R)

        if half == 0:
            pl.semaphore_wait(barrier, 46)
            core_copies = [
                send(part.at[0, :, :, p], core_in.at[p], core_ss.at[p], core_rs.at[p], sibling) for p in range(2)]
            sent += core_copies

    y_copies = []
    for p in range(2):
        core_copies[p].wait_recv()
        core_sum[p] = part[1, :, :, p] + core_in[p]
        copies = [
            send(core_sum.at[p, y_of(k)], y_in.at[p, k - 1], y_ss.at[p, k - 1], y_rs.at[p, k - 1], to_y(k))
            for k in (2, 1, 3)]
        y_copies.append(copies)
        sent += copies
    z_copies = []
    for p in range(2):
        for copy in y_copies[p]:
            copy.wait_recv()
        y_sum[p] = core_sum[p, y] + y_in[p, 0] + y_in[p, 1] + y_in[p, 2]
        copies = [
            send(y_sum.at[p, z_of(k)], z_in.at[p, k - 1], z_ss.at[p, k - 1], z_rs.at[p, k - 1], to_z(k))
            for k in (8, 7, 9, 6, 10, 5, 11, 4, 12, 3, 13, 2, 14, 1, 15)]
        z_copies.append(copies)
        sent += copies
    for p in range(2):
        for copy in z_copies[p]:
            copy.wait_recv()
        total = y_sum[p, col]
        for k in range(15):
            total = total + z_in[p, k]
        mine[p] = total
    rows16 = mine[...].reshape(16, R)
    rows_hi = rows16.astype(jnp.bfloat16)
    rows_lo = (rows16 - rows_hi.astype(jnp.float32)).astype(jnp.bfloat16)
    high[core, y, col] = rows_hi
    low[core, y, col] = rows_lo
    gathers = []
    for which, ref in enumerate((high, low)):
        copies = [
            send(ref.at[core, y, col], ref.at[core, y, col], hz_ss.at[which, k - 1], hz_rs.at[which, k - 1], to_z(k))
            for k in (8, 7, 9, 6, 10, 5, 11, 4, 12, 3, 13, 2, 14, 1, 15)]
        gathers.append(copies)
        sent += copies

    def spread(which, ref):
        for copy in gathers[which]:
            copy.wait_recv()
        return [
            send(ref.at[core, y], ref.at[core, y], hy_ss.at[which, k - 1], hy_rs.at[which, k - 1], to_y(k))
            for k in (2, 1, 3)]

    spreads = [spread(0, high)]
    sent += spreads[0]
    block = high[core, y].reshape(256, R)
    gram_part[...] = lax.dot_general(
        block, block, (((0,), (0,)), ((), ())), preferred_element_type=jnp.float32).reshape(4, 8, 8, R)
    gram_copies = []
    for k in range(1, 32):
        r, s = group_of(k)
        gram_copies.append(
            send(gram_part.at[r, s], gram_in.at[k - 1], g_ss.at[k - 1], g_rs.at[k - 1], to_group(k)))
    sent += gram_copies
    total = gram_part[row, section]
    for k in range(31):
        gram_copies[k].wait_recv()
        total = total + gram_in[k]
    gram_all[row, section] = total
    back_copies = [
        send(gram_all.at[row, section], gram_all.at[row, section], b_ss.at[k - 1], b_rs.at[k - 1], to_group(k))
        for k in range(1, 32)]
    sent += back_copies

    spreads.append(spread(1, low))
    sent += spreads[1]
    pairs = []
    for which, ref in enumerate((high, low)):
        for copy in spreads[which]:
            copy.wait_recv()
        pairs.append(send(ref.at[core], ref.at[core], hc_ss.at[which], hc_rs.at[which], sibling))
    sent += pairs
    for copy in back_copies:
        copy.wait_recv()
    gram_out[...] = gram_all[...].reshape(R, R)
    for copy in pairs:
        copy.wait_recv()
    outs = [
        pltpu.make_async_copy(high, hi_out, out_sem.at[0]),
        pltpu.make_async_copy(low, lo_out, out_sem.at[1]),
    ]
    for copy in outs:
        copy.start()
    for copy in sent:
        copy.wait_send()
    for copy in outs:
        copy.wait()


def summed(weights, sketch):
    f32, bf16, dma = jnp.float32, jnp.bfloat16, pltpu.SemaphoreType.DMA
    vmem = pl.BlockSpec(memory_space=pltpu.VMEM)
    hbm = pl.BlockSpec(memory_space=pl.ANY)
    full = jax.ShapeDtypeStruct((2, 4, 16, 16, R), bf16)
    return pl.pallas_call(
        sum_and_gram,
        out_shape=(full, full, jax.ShapeDtypeStruct((R, R), f32)),
        in_specs=[hbm, vmem],
        out_specs=(hbm, hbm, vmem),
        scratch_shapes=[
            pltpu.VMEM((2, 1024, 832), bf16),
            pltpu.VMEM((2, 4, 16, 2, 8, R), f32),
            pltpu.VMEM((2, 4, 16, 8, R), f32),
            pltpu.VMEM((2, 4, 16, 8, R), f32),
            pltpu.VMEM((2, 3, 16, 8, R), f32),
            pltpu.VMEM((2, 16, 8, R), f32),
            pltpu.VMEM((2, 15, 8, R), f32),
            pltpu.VMEM((2, 8, R), f32),
            pltpu.VMEM((2, 4, 16, 16, R), bf16),
            pltpu.VMEM((2, 4, 16, 16, R), bf16),
            pltpu.VMEM((4, 8, 8, R), f32),
            pltpu.VMEM((31, 8, R), f32),
            pltpu.VMEM((4, 8, 8, R), f32),
            dma((2,)), dma((2,)), dma((2,)), dma((2, 3)), dma((2, 3)), dma((2, 15)), dma((2, 15)),
            dma((2, 15)), dma((2, 15)), dma((2, 3)), dma((2, 3)), dma((2,)), dma((2,)),
            dma((31,)), dma((31,)), dma((31,)), dma((31,)), dma((2,)),
        ],
        compiler_params=pltpu.CompilerParams(
            collective_id=0, has_side_effects=True, vmem_limit_bytes=48 << 20),
    )(weights, sketch)


def invert_lower(gram_matrix):
    lower_factor = jnp.linalg.cholesky(gram_matrix)
    identity = jnp.eye(gram_matrix.shape[0], dtype=jnp.float32)
    return jax.scipy.linalg.solve_triangular(lower_factor, identity, lower=True)


def shards(weights, sketch):
    high, low, gram_matrix = summed(weights, sketch)
    sample = high.reshape(2048, R).astype(jnp.float32) + low.reshape(2048, R).astype(jnp.float32)
    inverse_factor = invert_lower(gram_matrix)
    product = jnp.dot(sample, inverse_factor.T, precision=lax.Precision.HIGHEST)
    shared_basis = (math.sqrt(D) * product).astype(jnp.bfloat16)
    product = lax.dot_general(
        shared_basis, weights, (((0,), (0,)), ((), ())), preferred_element_type=jnp.float32
    )
    coefficients = lax.psum_scatter(product / math.sqrt(D), "row", scatter_dimension=0, tiled=True)
    return (shared_basis, coefficients)


def solution(mesh):
    placed = (P("row", ("section", "col")), P(("section", "col"), None))
    return jax.shard_map(
        shards,
        mesh=mesh,
        in_specs=placed,
        out_specs=(P("row", None), P("row", ("section", "col"))),
        check_vma=False,
    )
```

time: 553 us -> 185 us (0.33)
  waiting for transfers between devices: 438 us -> 22.8 us
  Pallas kernels: 0 us -> 74.8 us
  matrix products: 22.5 us -> 5.43 us
  other arithmetic: 62.2 us -> 54.3 us
    psum x2 -> x0, waiting for transfers between devices: 406 us -> none  [the longest x1 353 us: shards(): sample = lax.psum(local_sample, ('section', 'col'))]
    pallas_call x0 -> x1, Pallas kernels: none -> 74.8 us  [summed(): pl.pallas_call(sum_and_gram, out_shape=(full, full, jax.ShapeDtypeStruct(...]
    dot_general x3 -> x1, matrix products: 13.4 us -> 1.84 us  [shards(): product = jnp.dot(sample, inverse_factor.T, precision=lax.Precision.HIGHEST)]
    reduce_scatter x1, waiting for transfers between devices: 32.1 us -> 22.8 us  [shards(): lax.psum_scatter(product / math.sqrt(D), 'row', scatter_dimension=0, tile...]
  transfers between devices with their start and end apart: 3 -> 1, of which waited for: 3 -> 1; matrix products, arithmetic and copies ran while one was open for 0% -> 0% of each run, Pallas kernels for 0% -> 0%
where the time goes in v1:
time: 185 us; the launch traced here: 183 us
  Pallas kernels  74.8 us (40%)
  other arithmetic  54.3 us (29%)
  waiting for transfers between devices  22.8 us (12%)
  between operations  15.5 us (8%)
  local copies, waits for them, and re-layouts  10.5 us (6%)
  matrix products  5.43 us (3%)
    pallas_call x1, Pallas kernels, summed(): pl.pallas_call(sum_and_gram, out_shape=(full, full, jax.ShapeDtypeStruct(...  74.8 us
    another operation x6, other arithmetic, invert_lower(): lower_factor = jnp.linalg.cholesky(gram_matrix)  34 us
    reduce_scatter x1, waiting for transfers between devices, shards(): lax.psum_scatter(product / math.sqrt(D), 'row', scatter_dimension=0, tile...  22.8 us
    another operation x3, other arithmetic, invert_lower(): return jax.scipy.linalg.solve_triangular(lower_factor, identity, lower=True)  19.9 us
    unnamed x7, local copies, waits for them, and re-layouts  6.22 us
    another operation x6, local copies, waits for them, and re-layouts  4.06 us
  transfers between devices with their start and end apart: 1, of which 1 were waited for; matrix products, arithmetic and copies ran while one was open for 0% of the time, Pallas kernels for 0%

profile of v1, /device:TPU:1, one launch (start us, length us, event | category | flops | bytes accessed | tf_op | source)
XLA Modules:
  0.0 183.5 jit_solution(13189242202655150059)
XLA Ops:
  7.3 6.1 %copy.4.w_hbm = bf16[2048,832]{1,0:T(8,128)(2,1)} copy(bf16[2048,832]{0,1:T(8,128)(2,1)} %param.2) | data formatting | bytes 6815744 | tf_op args[0]
  13.4 74.8 %shard_map.41 = (bf16[2,4,16,16,256]{4,3,2,1,0:T(8,128)(2,1)S(1)}, bf16[2,4,16,16,256]{4,3,2,1,0:T(8,128)(2,1)S(1)}, f32[256,256]{1,0:T(8,128)S(1)}) custom-call(bf16[2048,832]{1,0:T(8,128)(2,1)} %copy.4.w_hbm, bf16[832,256]{1,0:T(8,128)(2,1)S(1)} %copy-done), custom_call_target="tpu_custom_call" | custom-call | tf_op jit(solution)/shard_map/pallas_call | solution.py:180
  88.2 0.1 copy.5
  88.4 11.7 %cholesky.50 = f32[128,128]{1,0:T(8,128)S(1)} custom-call(f32[128,128]{1,0:T(8,128)S(1)} %cholesky.118), custom_call_target="Cholesky" | custom-call | tf_op jit(solution)/shard_map/jit(cholesky)/cholesky | solution.py:209
  100.1 9.8 %custom-call.15 = f32[1,128,128]{1,2,0:T(8,128)S(1)} custom-call(f32[1,128,128]{2,1,0:T(8,128)S(1)} %get-tuple-element.29), custom_call_target="InvertDiagBlocksLowerTriangular" | custom-call | tf_op jit(solution)/shard_map/jit(cholesky)/cholesky | solution.py:209
  109.9 0.2 constant_dynamic-update-slice_fusion.1
  110.2 0.3 convolution_subtract_fusion.1
  110.4 11.7 %cholesky.105 = f32[128,128]{1,0:T(8,128)S(1)} custom-call(f32[128,128]{1,0:T(8,128)S(1)} %convolution_subtract_fusion.1), custom_call_target="Cholesky" | custom-call | tf_op jit(solution)/shard_map/jit(cholesky)/cholesky | solution.py:209
  122.2 0.7 compare_reduce_fusion
  124.3 0.1 triangular_solve.63
  124.4 4.1 %while.1 = (s32[]{:T(128)}, f32[256,256]{1,0:T(8,128)S(1)}, s32[2,2]{1,0:T(2,128)S(1)}, f32[2,128,128]{2,1,0:T(8,128)S(1)}, s32[]{:T(128)}) while((s32[]{:T(128)}, f32[256,256]{1,0:T(8,128)S(1)}, s32[2,2]{1,0:T(2,128)S(1)}, f32[2,128,128]{2,1,0:T(8,128)S(1)}, s32[]{:T(128)}) %tuple.27), condition=%wide.while_cond, body=%wide.while_body.sunk | while | flops 2 | bytes 131181 | solution.py:211
  124.4 0.6 fusion.22
  125.0 1.4 bitcast_dynamic-update-slice_fusion.2
  126.4 0.6 fusion.22
  127.0 1.4 bitcast_dynamic-update-slice_fusion.2
  128.5 19.9 %custom-call.16 = f32[2,128,128]{1,2,0:T(8,128)S(1)} custom-call(f32[2,128,128]{2,1,0:T(8,128)S(1)} %get-tuple-element.15), custom_call_target="InvertDiagBlocksLowerTriangular" | custom-call | tf_op jit(solution)/shard_map/jit(_solve_triangular)/triangular_solve | solution.py:211
  148.4 0.3 fusion.5
  148.6 0.3 convolution_subtract_fusion
  148.9 0.3 fusion.8
  149.2 0.3 convert_add_fusion
  149.6 1.8 %fusion = bf16[2048,256]{1,0:T(8,128)(2,1)S(1)} fusion(f32[2048,256]{1,0:T(8,128)S(1)} %bitcast.35, f32[128,256]{1,0:T(8,128)S(1)} %fusion.8, f32[128,256]{1,0:T(8,128)S(1)} %fusion.5), kind=kOutput, calls=%fused_computation.3 | convolution fusion | flops 1611726848 | bytes 3407872 | tf_op jit(solution)/shard_map/dot_general | solution.py:218
  151.4 0.1 copy-done.1
  151.5 2.3 %convolution_multiply_fusion.1 = f32[256,832]{1,0:T(8,128)} fusion(bf16[2048,256]{1,0:T(8,128)(2,1)S(1)} %fusion, bf16[2048,832]{0,1:T(8,128)(2,1)S(1)} %copy-done.1), kind=kOutput, calls=%fused_computation.5 | convolution fusion | flops 872628224 | bytes 5308416 | tf_op jit(solution)/shard_map/dot_general | solution.py:220
  153.8 22.8 %reduce-scatter.2.cloned.1.call-done = f32[64,832]{1,0:T(8,128)} async-done(((f32[256,832]{1,0:T(8,128)}), f32[64,832]{1,0:T(8,128)}) %reduce-scatter.2.cloned.1.call-update) | async-done | bytes 213008 | tf_op jit(solution)/shard_map/reduce_scatter | solution.py:223
  (18 shorter events, 0.3 us)
Async XLA Ops:
  7.2 169.5 %reduce-scatter.2.cloned.1.call-start = ((), (), s32[]{:S(2)}) async-start(), calls=%async_computation.1 | async-start | bytes 1146880 | tf_op jit(solution)/shard_map/reduce_scatter | solution.py:223
  7.3 6.1 %copy-start = (bf16[832,256]{1,0:T(8,128)(2,1)S(1)}, bf16[832,256]{1,0:T(8,128)(2,1)}, u32[]{:S(2)}) copy-start(bf16[832,256]{1,0:T(8,128)(2,1)} %s_ref.1) | copy-start | bytes 1277956
  149.6 2.0 %copy-start.1 = (bf16[2048,832]{0,1:T(8,128)(2,1)S(1)}, bf16[2048,832]{0,1:T(8,128)(2,1)}, u32[]{:S(2)}) copy-start(bf16[2048,832]{0,1:T(8,128)(2,1)} %param.2) | copy-start | bytes 10223620
  151.5 2.3 %copy-start.2 = (bf16[2048,256]{1,0:T(8,128)(2,1)}, bf16[2048,256]{1,0:T(8,128)(2,1)S(1)}, u32[]{:S(2)}) copy-start(bf16[2048,256]{1,0:T(8,128)(2,1)S(1)} %fusion) | copy-start | bytes 3145732
Sparse Core Ops, SparseCore 0:
  153.9 22.6 reduce-scatter.1

commit v2 on v1

v2 whole, which is shorter than its diff:
```python
import math

import jax
import jax.numpy as jnp
from jax import lax
from jax.experimental import pallas as pl
from jax.experimental.pallas import tpu as pltpu
from jax.sharding import PartitionSpec as P

D = 8192
R = 256
WIDTH = 832
PAD = 896
PANEL = 32
PIECES = ((0, 256), (256, 256), (512, 320))
FAR_FIRST = (8, 7, 9, 6, 10, 5, 11, 4, 12, 3, 13, 2, 14, 1, 15)
MESH = pl.DeviceIdType.MESH
NT = (((1,), (1,)), ((), ()))


def split(x):
    high = x.astype(jnp.bfloat16)
    return high, (x - high.astype(jnp.float32)).astype(jnp.bfloat16)


def spread_lane(x, lane):
    return jnp.take_along_axis(x, jnp.full((8, 128), lane, jnp.int32), axis=1)


def factor_half(half, a, left, right):
    lane = lax.broadcasted_iota(jnp.int32, (8, 128), 1)
    sub = lax.broadcasted_iota(jnp.int32, (8, 128), 0)
    lane256 = lax.broadcasted_iota(jnp.int32, (PANEL, R), 1)
    sub256 = lax.broadcasted_iota(jnp.int32, (PANEL, R), 0)
    lanes = lax.broadcasted_iota(jnp.int32, (R, R), 1)
    subs = lax.broadcasted_iota(jnp.int32, (R, R), 0)
    groups = PANEL // 8
    mine, rest = slice(half * 128, half * 128 + 128), slice((1 - half) * 128, (1 - half) * 128 + 128)

    @pl.loop(0, 128 // PANEL)
    def _(q):
        base = half * 128 + q * PANEL
        rows = pl.ds(pl.multiple_of(base, PANEL), PANEL)
        factors = right[...]
        panel = jnp.where((lane256 >= base - PANEL) & (lane256 < base), 0.0, a[rows, :]) - jnp.dot(
            left[rows, :], factors, preferred_element_type=jnp.float32)
        old = (lanes >= base - PANEL) & (lanes < base) & (subs >= base)
        below = jnp.where(old, 0.0, a[...]) - jnp.dot(left[...], factors, preferred_element_type=jnp.float32)
        x = [panel[8 * g:8 * g + 8, mine] for g in range(groups)]
        z = [panel[8 * g:8 * g + 8, rest] for g in range(groups)]
        for b in range(groups):
            lane0 = q * PANEL + 8 * b
            inside = (lane >= lane0) & (lane < lane0 + 8)
            columns = {g: [spread_lane(x[g], lane0 + j) for j in range(8)] for g in range(b, groups)}
            s = {}
            for j in range(8):
                for i in range(j, 8):
                    s[i, j] = jnp.broadcast_to(columns[b][j][i:i + 1, :], (8, 128))
            u, v = [], []
            for i in range(8):
                spread = jnp.broadcast_to(x[b][i:i + 1, :], (8, 128))
                u.append(jnp.where(inside, jnp.where(lane == lane0 + i, 1.0, 0.0), spread))
                v.append(jnp.broadcast_to(z[b][i:i + 1, :], (8, 128)))
            for g in range(b + 1, groups):
                x[g] = jnp.where(inside, 0.0, x[g])
            for j in range(8):
                scale = lax.rsqrt(s[j, j])
                for i in range(j + 1, 8):
                    s[i, j] = s[i, j] * scale
                for i in range(j + 1, 8):
                    for k in range(j + 1, i + 1):
                        s[i, k] = s[i, k] - s[i, j] * s[k, j]
                u[j] = u[j] * scale
                v[j] = v[j] * scale
                for i in range(j + 1, 8):
                    u[i] = u[i] - s[i, j] * u[j]
                    v[i] = v[i] - s[i, j] * v[j]
                for g in range(b + 1, groups):
                    multiplier = columns[g][j] * scale
                    for k in range(j + 1, 8):
                        columns[g][k] = columns[g][k] - multiplier * s[k, j]
                    x[g] = x[g] - multiplier * u[j]
                    z[g] = z[g] - multiplier * v[j]
            x[b], z[b] = u[0], v[0]
            for i in range(1, 8):
                x[b] = jnp.where(sub == i, u[i], x[b])
                z[b] = jnp.where(sub == i, v[i], z[b])
        parts = [jnp.concatenate(x, axis=0), jnp.concatenate(z, axis=0)]
        new = jnp.concatenate(parts if half == 0 else parts[::-1], axis=1)
        a[...] = below
        a[rows, :] = new
        high, low = split(jnp.where((lane256 > base + sub256) & (lane256 < base + PANEL), 0.0, new))
        right[0:PANEL, :] = high
        right[PANEL:2 * PANEL, :] = low
        right[2 * PANEL:, :] = high
        high, low = split(jnp.where(lane256 >= base + PANEL, new, 0.0).T)
        left[:, 0:PANEL] = high
        left[:, PANEL:2 * PANEL] = high
        left[:, 2 * PANEL:] = low


def whole(w_hbm, s_ref, basis_out, coef_out, w_ref, st_ref, part, core_in, core_sum, y_in, y_sum, z_in, mine,
          high, low, gram_part, gram_in, gram_all, a, left, right, basis_t, coef, coef_send, coef_in,
          w_sem, core_ss, core_rs, y_ss, y_rs, z_ss, z_rs, hz_ss, hz_rs, hy_ss, hy_rs, hc_ss, hc_rs,
          g_ss, g_rs, b_ss, b_rs, c_ss, c_rs):
    section = lax.axis_index("section")
    row = lax.axis_index("row")
    col = lax.axis_index("col")
    core = lax.rem(section, 2)
    y = section // 2
    other = 1 - core
    sibling = {"section": 2 * y + other}

    def y_of(k):
        return lax.rem(y + k, 4)

    def z_of(k):
        return lax.rem(col + k, 16)

    def x_of(k):
        return lax.rem(row + k, 4)

    def to_y(k):
        return {"section": 2 * y_of(k) + core}

    def to_z(k):
        return {"col": z_of(k)}

    def group_of(k):
        return lax.rem(row + k // 8, 4), lax.rem(section + k % 8, 8)

    def to_group(k):
        r, s = group_of(k)
        return {"row": r, "section": s}

    sent = []

    def send(src, dst, ss, rs, device):
        copy = pltpu.make_async_remote_copy(
            src_ref=src, dst_ref=dst, send_sem=ss, recv_sem=rs, device_id=device, device_id_type=MESH)
        copy.start()
        sent.append(copy)
        return copy

    loads = []
    for half, which in enumerate((other, core)):
        load = pltpu.make_async_copy(
            w_hbm.at[:, pl.ds(pl.multiple_of(which * 1024, 1024), 1024)], w_ref.at[which], w_sem.at[half])
        load.start()
        loads.append(load)

    barrier = pltpu.get_barrier_semaphore()
    for k in range(1, 32):
        pl.semaphore_signal(barrier, inc=1, device_id=to_group(k), device_id_type=MESH)
    for k in range(1, 16):
        pl.semaphore_signal(barrier, inc=1, device_id=to_z(k), device_id_type=MESH)

    st_ref[...] = s_ref[...].T
    for half, which in enumerate((other, core)):
        loads[half].wait()
        for q in range(4):
            product = jnp.dot(
                st_ref[...], w_ref[which, :, q * 256:q * 256 + 256], preferred_element_type=jnp.float32)
            part[half, q] = product.reshape(16, 2, 8, R)
        if half == 0:
            pl.semaphore_wait(barrier, 46)
            core_copies = [
                send(part.at[0, :, :, p], core_in.at[p], core_ss.at[p], core_rs.at[p], sibling) for p in range(2)]

    y_copies = []
    for p in range(2):
        core_copies[p].wait_recv()
        core_sum[p] = part[1, :, :, p] + core_in[p]
        y_copies.append([
            send(core_sum.at[p, y_of(k)], y_in.at[p, k - 1], y_ss.at[p, k - 1], y_rs.at[p, k - 1], to_y(k))
            for k in (2, 1, 3)])
    z_copies = []
    for p in range(2):
        for copy in y_copies[p]:
            copy.wait_recv()
        y_sum[p] = core_sum[p, y] + y_in[p, 0] + y_in[p, 1] + y_in[p, 2]
        z_copies.append([
            send(y_sum.at[p, z_of(k)], z_in.at[p, k - 1], z_ss.at[p, k - 1], z_rs.at[p, k - 1], to_z(k))
            for k in FAR_FIRST])
    for p in range(2):
        for copy in z_copies[p]:
            copy.wait_recv()
        total = y_sum[p, col]
        for k in range(15):
            total = total + z_in[p, k]
        mine[p] = total
    high[core, y, col], low[core, y, col] = split(mine[...].reshape(16, R))
    gathers = [
        [send(ref.at[core, y, col], ref.at[core, y, col], hz_ss.at[which, k - 1], hz_rs.at[which, k - 1], to_z(k))
         for k in FAR_FIRST]
        for which, ref in enumerate((high, low))]

    def spread(which, ref):
        return [
            send(ref.at[core, y], ref.at[core, y], hy_ss.at[which, k - 1], hy_rs.at[which, k - 1], to_y(k))
            for k in (2, 1, 3)]

    def pair(which, ref):
        return send(ref.at[core], ref.at[core], hc_ss.at[which], hc_rs.at[which], sibling)

    def arrive(copies):
        for copy in copies:
            copy.wait_recv()

    arrive(gathers[0])
    block = high[core, y].reshape(R, R)
    gram_part[...] = lax.dot_general(block, block, NT, preferred_element_type=jnp.float32).reshape(4, 8, 8, R)
    gram_copies = []
    for k in range(1, 32):
        r, s = group_of(k)
        gram_copies.append(
            send(gram_part.at[r, s], gram_in.at[k - 1], g_ss.at[k - 1], g_rs.at[k - 1], to_group(k)))
    spread_high = spread(0, high)
    total = gram_part[row, section]
    for k in range(31):
        gram_copies[k].wait_recv()
        total = total + gram_in[k]
    gram_all[row, section] = total
    back_copies = [
        send(gram_all.at[row, section], gram_all.at[row, section], b_ss.at[k - 1], b_rs.at[k - 1], to_group(k))
        for k in range(1, 32)]

    arrive(gathers[1])
    spread_low = spread(1, low)
    coef_send[:, :, 768:] = jnp.zeros((4, 64, PAD - 768), jnp.bfloat16)
    left[...] = jnp.zeros_like(left)
    right[...] = jnp.zeros_like(right)
    arrive(spread_high)
    pair_high = pair(0, high)
    arrive(back_copies)
    a[...] = gram_all[...].reshape(R, R)
    factor_half(0, a, left, right)
    arrive(spread_low)
    pair_low = pair(1, low)
    factor_half(1, a, left, right)

    lower = lax.broadcasted_iota(jnp.int32, (R, R), 0) >= lax.broadcasted_iota(jnp.int32, (R, R), 1)
    inverse_high, inverse_low = split(jnp.where(lower, a[...] * math.sqrt(D), 0.0))
    arrive([pair_high, pair_low])

    def dot(p, q):
        return jnp.dot(p, q, preferred_element_type=jnp.float32)

    for c in range(2):
        for q in range(4):
            block_high = high[c, q].reshape(R, R)
            block_low = low[c, q].reshape(R, R)
            product = dot(inverse_high, block_high) + (dot(inverse_high, block_low) + dot(inverse_low, block_high))
            basis_t[c, :, q * 256:q * 256 + 256] = product.astype(jnp.bfloat16)
    coef_copies = []
    for piece, (first, width) in enumerate(PIECES):
        product = jnp.zeros((R, width), jnp.float32)
        for c in range(2):
            product = product + lax.dot_general(
                basis_t[c], w_ref[c, first:first + width, :], NT, preferred_element_type=jnp.float32)
        product = product.reshape(4, 64, width)
        coef[:, :, first:first + width] = product
        coef_send[:, :, first:first + width] = product.astype(jnp.bfloat16)
        lanes = pl.ds(first, width if piece < 2 else PAD - first)
        coef_copies.append([
            send(coef_send.at[x_of(k), :, lanes], coef_in.at[k - 1, :, lanes], c_ss.at[piece, k - 1],
                 c_rs.at[piece, k - 1], {"row": x_of(k)})
            for k in (2, 1, 3)])
    for c in range(2):
        for q in range(4):
            first = c * 1024 + q * 256
            basis_out[first:first + 256, :] = basis_t[c, :, q * 256:q * 256 + 256].T
    for piece, (first, width) in enumerate(PIECES):
        arrive(coef_copies[piece])
        total = coef[row, :, first:first + width]
        for k in range(3):
            total = total + coef_in[k, :, first:first + width].astype(jnp.float32)
        coef_out[:, first:first + width] = total / math.sqrt(D)
    for copy in sent:
        copy.wait_send()


def shards(weights, sketch):
    f32, bf16, dma = jnp.float32, jnp.bfloat16, pltpu.SemaphoreType.DMA
    vmem = pl.BlockSpec(memory_space=pltpu.VMEM)
    return pl.pallas_call(
        whole,
        out_shape=(jax.ShapeDtypeStruct((2048, R), bf16), jax.ShapeDtypeStruct((64, WIDTH), f32)),
        in_specs=[pl.BlockSpec(memory_space=pl.ANY), vmem],
        out_specs=(vmem, vmem),
        scratch_shapes=[
            pltpu.VMEM((2, WIDTH, 1024), bf16),
            pltpu.VMEM((R, WIDTH), bf16),
            pltpu.VMEM((2, 4, 16, 2, 8, R), f32),
            pltpu.VMEM((2, 4, 16, 8, R), f32),
            pltpu.VMEM((2, 4, 16, 8, R), f32),
            pltpu.VMEM((2, 3, 16, 8, R), f32),
            pltpu.VMEM((2, 16, 8, R), f32),
            pltpu.VMEM((2, 15, 8, R), f32),
            pltpu.VMEM((2, 8, R), f32),
            pltpu.VMEM((2, 4, 16, 16, R), bf16),
            pltpu.VMEM((2, 4, 16, 16, R), bf16),
            pltpu.VMEM((4, 8, 8, R), f32),
            pltpu.VMEM((31, 8, R), f32),
            pltpu.VMEM((4, 8, 8, R), f32),
            pltpu.VMEM((R, R), f32),
            pltpu.VMEM((R, 3 * PANEL), bf16),
            pltpu.VMEM((3 * PANEL, R), bf16),
            pltpu.VMEM((2, R, 1024), bf16),
            pltpu.VMEM((4, 64, WIDTH), f32),
            pltpu.VMEM((4, 64, PAD), bf16),
            pltpu.VMEM((3, 64, PAD), bf16),
            dma((2,)), dma((2,)), dma((2,)), dma((2, 3)), dma((2, 3)), dma((2, 15)), dma((2, 15)),
            dma((2, 15)), dma((2, 15)), dma((2, 3)), dma((2, 3)), dma((2,)), dma((2,)),
            dma((31,)), dma((31,)), dma((31,)), dma((31,)), dma((3, 3)), dma((3, 3)),
        ],
        compiler_params=pltpu.CompilerParams(
            collective_id=0, has_side_effects=True, vmem_limit_bytes=60 << 20),
    )(weights.T, sketch)


def solution(mesh):
    placed = (P("row", ("section", "col")), P(("section", "col"), None))
    return jax.shard_map(
        shards,
        mesh=mesh,
        in_specs=placed,
        out_specs=(P("row", None), P("row", ("section", "col"))),
        check_vma=False,
    )
```

time: 185 us -> 92.4 us (0.50)
  other arithmetic: 54.3 us -> 0 us
  waiting for transfers between devices: 22.8 us -> 0 us
  between operations: 15.5 us -> 0.64 us
  Pallas kernels: 74.8 us -> 87.6 us
  local copies, waits for them, and re-layouts: 10.5 us -> 3.9 us
  matrix products: 5.43 us -> 0 us
    another operation x9 -> x0, other arithmetic: 54 us -> none  [the longest x6 34 us: invert_lower(): lower_factor = jnp.linalg.cholesky(gram_matrix)]
    reduce_scatter x1 -> x0, waiting for transfers between devices: 22.8 us -> none  [shards(): lax.psum_scatter(product / math.sqrt(D), 'row', scatter_dimension=0, tile...]
    pallas_call x1, Pallas kernels: 74.8 us -> 87.6 us  [shards(): pl.pallas_call(whole, out_shape=(jax.ShapeDtypeStruct((2048, R), bf16), j...]
    another operation x9 -> x0, local copies, waits for them, and re-layouts: 4.16 us -> none
    dot_general x2 -> x0, matrix products: 4.12 us -> none  [the longest x1 2.28 us: shards(): lax.dot_general(shared_basis, weights, (((0,), (0,)), ((), ())), preferre...]
    unnamed x7 -> x2, local copies, waits for them, and re-layouts: 6.22 us -> 3.9 us
  transfers between devices with their start and end apart: 1 -> 0, of which waited for: 1 -> 0; matrix products, arithmetic and copies ran while one was open for 0% -> 0% of each run, Pallas kernels for 0% -> 0%
where the time goes in v2:
time: 92.4 us; the launch traced here: 92.2 us
  Pallas kernels  87.6 us (95%)
  local copies, waits for them, and re-layouts  3.9 us (4%)
    pallas_call x1, Pallas kernels, shards(): pl.pallas_call(whole, out_shape=(jax.ShapeDtypeStruct((2048, R), bf16), j...  87.6 us
    unnamed x2, local copies, waits for them, and re-layouts  3.9 us

profile of v2, /device:TPU:1, one launch (start us, length us, event | category | flops | bytes accessed | tf_op | source)
XLA Modules:
  0.0 92.2 jit_solution(12648174048192596036)
XLA Ops:
  0.6 87.6 %shard_map.41 = (bf16[2048,256]{1,0:T(8,128)(2,1)}, f32[64,832]{1,0:T(8,128)}) custom-call(bf16[832,2048]{1,0:T(8,128)(2,1)} %bitcast.1, bf16[832,256]{1,0:T(8,128)(2,1)} %s_ref.1), custom_call_target="tpu_custom_call" | custom-call | tf_op jit(solution)/shard_map/pallas_call | solution.py:286
  88.3 2.3 %copy.6 = bf16[2048,256]{1,0:T(8,128)(2,1)} copy(bf16[2048,256]{1,0:T(8,128)(2,1)} %get-tuple-element.4) | data formatting | bytes 2097152
  90.5 1.6 %copy.7 = f32[64,832]{1,0:T(8,128)} copy(f32[64,832]{1,0:T(8,128)} %get-tuple-element.5) | data formatting | bytes 425984

commit v3 on v2

--- a/solution.py
+++ b/solution.py
@@ -11,8 +11,10 @@
 R = 256
 WIDTH = 832
 PAD = 896
-PANEL = 32
+PANEL = 64
 PIECES = ((0, 256), (256, 256), (512, 320))
+QUARTERS = ((0, 0), (0, 1), (1, 0), (1, 1))
+GROUP = tuple(sorted(range(1, 32), key=lambda k: -(2 * min(k // 8, 4 - k // 8) + min(k % 8, 8 - k % 8))))
 FAR_FIRST = (8, 7, 9, 6, 10, 5, 11, 4, 12, 3, 13, 2, 14, 1, 15)
 MESH = pl.DeviceIdType.MESH
 NT = (((1,), (1,)), ((), ()))
@@ -99,9 +101,9 @@
         left[:, 2 * PANEL:] = low
 
 
-def whole(w_hbm, s_ref, basis_out, coef_out, w_ref, st_ref, part, core_in, core_sum, y_in, y_sum, z_in, mine,
-          high, low, gram_part, gram_in, gram_all, a, left, right, basis_t, coef, coef_send, coef_in,
-          w_sem, core_ss, core_rs, y_ss, y_rs, z_ss, z_rs, hz_ss, hz_rs, hy_ss, hy_rs, hc_ss, hc_rs,
+def whole(w_hbm, s_hbm, basis_out, coef_out, w_ref, s_ref, st_ref, part, core_in, core_sum, y_in, y_sum, z_in,
+          rows, gram_part, gram_in, gram_all, a, left, right, basis_t, coef, coef_send, coef_in,
+          w_sem, core_ss, core_rs, y_ss, y_rs, z_ss, z_rs, h_ss, h_rs, hy_ss, hy_rs, hc_ss, hc_rs,
           g_ss, g_rs, b_ss, b_rs, c_ss, c_rs):
     section = lax.axis_index("section")
     row = lax.axis_index("row")
@@ -133,125 +135,136 @@
         r, s = group_of(k)
         return {"row": r, "section": s}
 
-    sent = []
+    sent, pending = [], []
 
     def send(src, dst, ss, rs, device):
         copy = pltpu.make_async_remote_copy(
             src_ref=src, dst_ref=dst, send_sem=ss, recv_sem=rs, device_id=device, device_id_type=MESH)
         copy.start()
         sent.append(copy)
+        pending.append(copy)
         return copy
 
-    loads = []
+    def arrive(copies):
+        for copy in copies:
+            copy.wait_recv()
+            pending[:] = [c for c in pending if c is not copy]
+
+    barrier = pltpu.get_barrier_semaphore()
+    for k in range(1, 32):
+        pl.semaphore_signal(barrier, inc=1, device_id=to_group(k), device_id_type=MESH)
+    for k in range(1, 16):
+        pl.semaphore_signal(barrier, inc=1, device_id=to_z(k), device_id_type=MESH)
+
+    loads, core_copies = [], []
+    load_s = pltpu.make_async_copy(s_hbm, s_ref, w_sem.at[2])
+    load_s.start()
     for half, which in enumerate((other, core)):
         load = pltpu.make_async_copy(
             w_hbm.at[:, pl.ds(pl.multiple_of(which * 1024, 1024), 1024)], w_ref.at[which], w_sem.at[half])
         load.start()
         loads.append(load)
 
-    barrier = pltpu.get_barrier_semaphore()
-    for k in range(1, 32):
-        pl.semaphore_signal(barrier, inc=1, device_id=to_group(k), device_id_type=MESH)
-    for k in range(1, 16):
-        pl.semaphore_signal(barrier, inc=1, device_id=to_z(k), device_id_type=MESH)
-
+    load_s.wait()
     st_ref[...] = s_ref[...].T
     for half, which in enumerate((other, core)):
         loads[half].wait()
-        for q in range(4):
+        for p in range(2):
             product = jnp.dot(
-                st_ref[...], w_ref[which, :, q * 256:q * 256 + 256], preferred_element_type=jnp.float32)
-            part[half, q] = product.reshape(16, 2, 8, R)
-        if half == 0:
-            pl.semaphore_wait(barrier, 46)
-            core_copies = [
-                send(part.at[0, :, :, p], core_in.at[p], core_ss.at[p], core_rs.at[p], sibling) for p in range(2)]
-
+                st_ref[...], w_ref[which, :, p * 512:p * 512 + 512], preferred_element_type=jnp.float32)
+            for q in range(4):
+                part[half, p, q] = product[:, q * 128:q * 128 + 128].reshape(16, 2, 8, 128)
+            if half == 0:
+                if p == 0:
+                    pl.semaphore_wait(barrier, 46)
+                core_copies.append(send(part.at[0, p], core_in.at[p], core_ss.at[p], core_rs.at[p], sibling))
     y_copies = []
-    for p in range(2):
-        core_copies[p].wait_recv()
-        core_sum[p] = part[1, :, :, p] + core_in[p]
+    for p, r in QUARTERS:
+        if r == 0:
+            arrive([core_copies[p]])
+        core_sum[p, r] = part[1, p, :, :, r] + core_in[p, :, :, r]
         y_copies.append([
-            send(core_sum.at[p, y_of(k)], y_in.at[p, k - 1], y_ss.at[p, k - 1], y_rs.at[p, k - 1], to_y(k))
+            send(core_sum.at[p, r, y_of(k)], y_in.at[p, r, k - 1], y_ss.at[p, r, k - 1], y_rs.at[p, r, k - 1], to_y(k))
             for k in (2, 1, 3)])
     z_copies = []
+    for quarter, (p, r) in enumerate(QUARTERS):
+        arrive(y_copies[quarter])
+        y_sum[p, r] = core_sum[p, r, y] + y_in[p, r, 0] + y_in[p, r, 1] + y_in[p, r, 2]
+        z_copies.append([
+            send(y_sum.at[p, r, z_of(k)], z_in.at[p, r, k - 1], z_ss.at[p, r, k - 1], z_rs.at[p, r, k - 1], to_z(k))
+            for k in FAR_FIRST])
+    gathers = []
+    for quarter, (p, r) in enumerate(QUARTERS):
+        arrive(z_copies[quarter])
+        total = y_sum[p, r, col]
+        for k in range(15):
+            total = total + z_in[p, r, k]
+        rows[core, p, y, col, r] = total
+        gathers.append([
+            send(rows.at[core, p, y, col, r], rows.at[core, p, y, col, r], h_ss.at[p, r, k - 1], h_rs.at[p, r, k - 1],
+                 to_z(k))
+            for k in FAR_FIRST])
+
+    def spread(p):
+        return [
+            send(rows.at[core, p, y], rows.at[core, p, y], hy_ss.at[p, k - 1], hy_rs.at[p, k - 1], to_y(k))
+            for k in (2, 1, 3)]
+
+    def pair(p):
+        return send(rows.at[core, p], rows.at[core, p], hc_ss.at[p], hc_rs.at[p], sibling)
+
+    gram = jnp.zeros((R, R), jnp.float32)
+    spreads = []
     for p in range(2):
-        for copy in y_copies[p]:
-            copy.wait_recv()
-        y_sum[p] = core_sum[p, y] + y_in[p, 0] + y_in[p, 1] + y_in[p, 2]
-        z_copies.append([
-            send(y_sum.at[p, z_of(k)], z_in.at[p, k - 1], z_ss.at[p, k - 1], z_rs.at[p, k - 1], to_z(k))
-            for k in FAR_FIRST])
-    for p in range(2):
-        for copy in z_copies[p]:
-            copy.wait_recv()
-        total = y_sum[p, col]
-        for k in range(15):
-            total = total + z_in[p, k]
-        mine[p] = total
-    high[core, y, col], low[core, y, col] = split(mine[...].reshape(16, R))
-    gathers = [
-        [send(ref.at[core, y, col], ref.at[core, y, col], hz_ss.at[which, k - 1], hz_rs.at[which, k - 1], to_z(k))
-         for k in FAR_FIRST]
-        for which, ref in enumerate((high, low))]
-
-    def spread(which, ref):
-        return [
-            send(ref.at[core, y], ref.at[core, y], hy_ss.at[which, k - 1], hy_rs.at[which, k - 1], to_y(k))
-            for k in (2, 1, 3)]
-
-    def pair(which, ref):
-        return send(ref.at[core], ref.at[core], hc_ss.at[which], hc_rs.at[which], sibling)
-
-    def arrive(copies):
-        for copy in copies:
-            copy.wait_recv()
-
-    arrive(gathers[0])
-    block = high[core, y].reshape(R, R)
-    gram_part[...] = lax.dot_general(block, block, NT, preferred_element_type=jnp.float32).reshape(4, 8, 8, R)
-    gram_copies = []
-    for k in range(1, 32):
+        arrive(gathers[2 * p])
+        arrive(gathers[2 * p + 1])
+        if p == 0:
+            spreads.append(spread(0))
+        high, low = split(rows[core, p, y].reshape(R, 128))
+        gram = gram + (lax.dot_general(high, high, NT, preferred_element_type=jnp.float32) + (
+            lax.dot_general(high, low, NT, preferred_element_type=jnp.float32) +
+            lax.dot_general(low, high, NT, preferred_element_type=jnp.float32)))
+    gram_part[...] = gram.reshape(4, 8, 8, R)
+    gram_copies = {}
+    for k in GROUP:
         r, s = group_of(k)
-        gram_copies.append(
-            send(gram_part.at[r, s], gram_in.at[k - 1], g_ss.at[k - 1], g_rs.at[k - 1], to_group(k)))
-    spread_high = spread(0, high)
+        gram_copies[k] = send(gram_part.at[r, s], gram_in.at[k - 1], g_ss.at[k - 1], g_rs.at[k - 1], to_group(k))
     total = gram_part[row, section]
-    for k in range(31):
-        gram_copies[k].wait_recv()
-        total = total + gram_in[k]
+    for k in GROUP[::-1]:
+        arrive([gram_copies[k]])
+        total = total + gram_in[k - 1]
     gram_all[row, section] = total
     back_copies = [
         send(gram_all.at[row, section], gram_all.at[row, section], b_ss.at[k - 1], b_rs.at[k - 1], to_group(k))
-        for k in range(1, 32)]
-
-    arrive(gathers[1])
-    spread_low = spread(1, low)
+        for k in GROUP]
+    spreads.append(spread(1))
     coef_send[:, :, 768:] = jnp.zeros((4, 64, PAD - 768), jnp.bfloat16)
     left[...] = jnp.zeros_like(left)
     right[...] = jnp.zeros_like(right)
-    arrive(spread_high)
-    pair_high = pair(0, high)
+    arrive(spreads[0])
+    pairs = [pair(0)]
     arrive(back_copies)
     a[...] = gram_all[...].reshape(R, R)
     factor_half(0, a, left, right)
-    arrive(spread_low)
-    pair_low = pair(1, low)
+    arrive(spreads[1])
+    pairs.append(pair(1))
     factor_half(1, a, left, right)
 
     lower = lax.broadcasted_iota(jnp.int32, (R, R), 0) >= lax.broadcasted_iota(jnp.int32, (R, R), 1)
     inverse_high, inverse_low = split(jnp.where(lower, a[...] * math.sqrt(D), 0.0))
-    arrive([pair_high, pair_low])
+    arrive(pairs)
 
     def dot(p, q):
         return jnp.dot(p, q, preferred_element_type=jnp.float32)
 
     for c in range(2):
-        for q in range(4):
-            block_high = high[c, q].reshape(R, R)
-            block_low = low[c, q].reshape(R, R)
-            product = dot(inverse_high, block_high) + (dot(inverse_high, block_low) + dot(inverse_low, block_high))
-            basis_t[c, :, q * 256:q * 256 + 256] = product.astype(jnp.bfloat16)
+        for p in range(2):
+            for q in range(0, 4, 2):
+                block = jnp.concatenate([rows[c, p, q].reshape(R, 128), rows[c, p, q + 1].reshape(R, 128)], axis=1)
+                high, low = split(block)
+                product = dot(inverse_high, high) + (dot(inverse_high, low) + dot(inverse_low, high))
+                first = p * 512 + q * 128
+                basis_t[c, :, first:first + 256] = product.astype(jnp.bfloat16)
     coef_copies = []
     for piece, (first, width) in enumerate(PIECES):
         product = jnp.zeros((R, width), jnp.float32)
@@ -286,20 +299,19 @@
     return pl.pallas_call(
         whole,
         out_shape=(jax.ShapeDtypeStruct((2048, R), bf16), jax.ShapeDtypeStruct((64, WIDTH), f32)),
-        in_specs=[pl.BlockSpec(memory_space=pl.ANY), vmem],
+        in_specs=[pl.BlockSpec(memory_space=pltpu.HBM)] * 2,
         out_specs=(vmem, vmem),
         scratch_shapes=[
             pltpu.VMEM((2, WIDTH, 1024), bf16),
+            pltpu.VMEM((WIDTH, R), bf16),
             pltpu.VMEM((R, WIDTH), bf16),
-            pltpu.VMEM((2, 4, 16, 2, 8, R), f32),
-            pltpu.VMEM((2, 4, 16, 8, R), f32),
-            pltpu.VMEM((2, 4, 16, 8, R), f32),
-            pltpu.VMEM((2, 3, 16, 8, R), f32),
-            pltpu.VMEM((2, 16, 8, R), f32),
-            pltpu.VMEM((2, 15, 8, R), f32),
-            pltpu.VMEM((2, 8, R), f32),
-            pltpu.VMEM((2, 4, 16, 16, R), bf16),
-            pltpu.VMEM((2, 4, 16, 16, R), bf16),
+            pltpu.VMEM((2, 2, 4, 16, 2, 8, 128), f32),
+            pltpu.VMEM((2, 4, 16, 2, 8, 128), f32),
+            pltpu.VMEM((2, 2, 4, 16, 8, 128), f32),
+            pltpu.VMEM((2, 2, 3, 16, 8, 128), f32),
+            pltpu.VMEM((2, 2, 16, 8, 128), f32),
+            pltpu.VMEM((2, 2, 15, 8, 128), f32),
+            pltpu.VMEM((2, 2, 4, 16, 2, 8, 128), f32),
             pltpu.VMEM((4, 8, 8, R), f32),
             pltpu.VMEM((31, 8, R), f32),
             pltpu.VMEM((4, 8, 8, R), f32),
@@ -310,12 +322,12 @@
             pltpu.VMEM((4, 64, WIDTH), f32),
             pltpu.VMEM((4, 64, PAD), bf16),
             pltpu.VMEM((3, 64, PAD), bf16),
-            dma((2,)), dma((2,)), dma((2,)), dma((2, 3)), dma((2, 3)), dma((2, 15)), dma((2, 15)),
-            dma((2, 15)), dma((2, 15)), dma((2, 3)), dma((2, 3)), dma((2,)), dma((2,)),
+            dma((3,)), dma((2,)), dma((2,)), dma((2, 2, 3)), dma((2, 2, 3)), dma((2, 2, 15)), dma((2, 2, 15)),
+            dma((2, 2, 15)), dma((2, 2, 15)), dma((2, 3)), dma((2, 3)), dma((2,)), dma((2,)),
             dma((31,)), dma((31,)), dma((31,)), dma((31,)), dma((3, 3)), dma((3, 3)),
         ],
         compiler_params=pltpu.CompilerParams(
-            collective_id=0, has_side_effects=True, vmem_limit_bytes=60 << 20),
+            collective_id=0, has_side_effects=True, vmem_limit_bytes=51 << 20),
     )(weights.T, sketch)
 
 

time: 92.4 us -> 87.3 us (0.945)
  Pallas kernels: 87.6 us -> 83.9 us
  local copies, waits for them, and re-layouts: 3.9 us -> 2.66 us
    pallas_call x1, Pallas kernels: 87.6 us -> 83.9 us  [shards(): pl.pallas_call(whole, out_shape=(jax.ShapeDtypeStruct((2048, R), bf16), j...]
    unnamed x2 -> x4, local copies, waits for them, and re-layouts: 3.9 us -> 2.66 us
where the time goes in v3:
time: 87.3 us; the launch traced here: 87.2 us
  Pallas kernels  83.9 us (96%)
  local copies, waits for them, and re-layouts  2.66 us (3%)
    pallas_call x1, Pallas kernels, shards(): pl.pallas_call(whole, out_shape=(jax.ShapeDtypeStruct((2048, R), bf16), j...  83.9 us
    unnamed x4, local copies, waits for them, and re-layouts  2.66 us

profile of v3, /device:TPU:1, one launch (start us, length us, event | category | flops | bytes accessed | tf_op | source)
XLA Modules:
  0.0 87.2 jit_solution(16236216746013447854)
XLA Ops:
  0.6 0.0 copy-start
  0.6 1.0 %copy-done = bf16[832,256]{1,0:T(8,128)(2,1)S(1)} copy-done((bf16[832,256]{1,0:T(8,128)(2,1)S(1)}, bf16[832,256]{1,0:T(8,128)(2,1)}, u32[]{:S(2)}) %copy-start) | copy-done | bytes 426008
  1.6 83.9 %shard_map.41 = (bf16[2048,256]{1,0:T(8,128)(2,1)S(1)}, f32[64,832]{1,0:T(8,128)S(1)}) custom-call(bf16[832,2048]{1,0:T(8,128)(2,1)} %bitcast.1, bf16[832,256]{1,0:T(8,128)(2,1)S(1)} %copy-done), custom_call_target="tpu_custom_call" | custom-call | tf_op jit(solution)/shard_map/pallas_call | solution.py:299
  85.5 1.0 %copy.6 = bf16[2048,256]{1,0:T(8,128)(2,1)} copy(bf16[2048,256]{1,0:T(8,128)(2,1)S(1)} %get-tuple-element.4) | data formatting | bytes 2097152
  86.5 0.7 copy.7
Async XLA Ops:
  0.6 1.0 %copy-start = (bf16[832,256]{1,0:T(8,128)(2,1)S(1)}, bf16[832,256]{1,0:T(8,128)(2,1)}, u32[]{:S(2)}) copy-start(bf16[832,256]{1,0:T(8,128)(2,1)} %s_hbm.1) | copy-start | bytes 1277956

commit v4 on v3

--- a/solution.py
+++ b/solution.py
@@ -177,12 +177,13 @@
             if half == 0:
                 if p == 0:
                     pl.semaphore_wait(barrier, 46)
-                core_copies.append(send(part.at[0, p], core_in.at[p], core_ss.at[p], core_rs.at[p], sibling))
+                core_copies += [
+                    send(part.at[0, p, :, :, r], core_in.at[p, r], core_ss.at[p, r], core_rs.at[p, r], sibling)
+                    for r in range(2)]
     y_copies = []
-    for p, r in QUARTERS:
-        if r == 0:
-            arrive([core_copies[p]])
-        core_sum[p, r] = part[1, p, :, :, r] + core_in[p, :, :, r]
+    for quarter, (p, r) in enumerate(QUARTERS):
+        arrive([core_copies[quarter]])
+        core_sum[p, r] = part[1, p, :, :, r] + core_in[p, r]
         y_copies.append([
             send(core_sum.at[p, r, y_of(k)], y_in.at[p, r, k - 1], y_ss.at[p, r, k - 1], y_rs.at[p, r, k - 1], to_y(k))
             for k in (2, 1, 3)])
@@ -298,7 +299,7 @@
     vmem = pl.BlockSpec(memory_space=pltpu.VMEM)
     return pl.pallas_call(
         whole,
-        out_shape=(jax.ShapeDtypeStruct((2048, R), bf16), jax.ShapeDtypeStruct((64, WIDTH), f32)),
+        out_shape=(pltpu.VMEM((2048, R), bf16), pltpu.VMEM((64, WIDTH), f32)),
         in_specs=[pl.BlockSpec(memory_space=pltpu.HBM)] * 2,
         out_specs=(vmem, vmem),
         scratch_shapes=[
@@ -306,7 +307,7 @@
             pltpu.VMEM((WIDTH, R), bf16),
             pltpu.VMEM((R, WIDTH), bf16),
             pltpu.VMEM((2, 2, 4, 16, 2, 8, 128), f32),
-            pltpu.VMEM((2, 4, 16, 2, 8, 128), f32),
+            pltpu.VMEM((2, 2, 4, 16, 8, 128), f32),
             pltpu.VMEM((2, 2, 4, 16, 8, 128), f32),
             pltpu.VMEM((2, 2, 3, 16, 8, 128), f32),
             pltpu.VMEM((2, 2, 16, 8, 128), f32),
@@ -322,12 +323,12 @@
             pltpu.VMEM((4, 64, WIDTH), f32),
             pltpu.VMEM((4, 64, PAD), bf16),
             pltpu.VMEM((3, 64, PAD), bf16),
-            dma((3,)), dma((2,)), dma((2,)), dma((2, 2, 3)), dma((2, 2, 3)), dma((2, 2, 15)), dma((2, 2, 15)),
+            dma((3,)), dma((2, 2)), dma((2, 2)), dma((2, 2, 3)), dma((2, 2, 3)), dma((2, 2, 15)), dma((2, 2, 15)),
             dma((2, 2, 15)), dma((2, 2, 15)), dma((2, 3)), dma((2, 3)), dma((2,)), dma((2,)),
-            dma((31,)), dma((31,)), dma((31,)), dma((31,)), dma((3, 3)), dma((3, 3)),
+            dma((31,)), dma((31,)), dma((31,)), dma((31,)), dma((4, 3)), dma((4, 3)),
         ],
         compiler_params=pltpu.CompilerParams(
-            collective_id=0, has_side_effects=True, vmem_limit_bytes=51 << 20),
+            collective_id=0, has_side_effects=True, vmem_limit_bytes=54 << 20),
     )(weights.T, sketch)
 
 

time: 87.3 us -> 86.3 us (0.989)
  local copies, waits for them, and re-layouts: 2.66 us -> 1.66 us
    unnamed x4 -> x2, local copies, waits for them, and re-layouts: 2.66 us -> 1.66 us
where the time goes in v4:
time: 86.3 us; the launch traced here: 86.2 us
  Pallas kernels  83.9 us (97%)
  local copies, waits for them, and re-layouts  1.66 us (2%)
    pallas_call x1, Pallas kernels, shards(): pl.pallas_call(whole, out_shape=(pltpu.VMEM((2048, R), bf16), pltpu.VMEM(...  83.9 us

profile of v4, /device:TPU:1, one launch (start us, length us, event | category | flops | bytes accessed | tf_op | source)
XLA Modules:
  0.0 86.2 jit_solution(11582334957810313756)
XLA Ops:
  0.6 83.9 %shard_map.41 = (bf16[2048,256]{1,0:T(8,128)(2,1)S(1)}, f32[64,832]{1,0:T(8,128)S(1)}) custom-call(bf16[832,2048]{1,0:T(8,128)(2,1)} %bitcast.1, bf16[832,256]{1,0:T(8,128)(2,1)} %s_hbm.1), custom_call_target="tpu_custom_call" | custom-call | tf_op jit(solution)/shard_map/pallas_call | solution.py:300
  84.6 1.0 %copy.6 = bf16[2048,256]{1,0:T(8,128)(2,1)} copy(bf16[2048,256]{1,0:T(8,128)(2,1)S(1)} %get-tuple-element.2) | data formatting | bytes 2097152
  85.5 0.7 copy.7

commit v5 on v4

--- a/solution.py
+++ b/solution.py
@@ -12,7 +12,7 @@
 WIDTH = 832
 PAD = 896
 PANEL = 64
-PIECES = ((0, 256), (256, 256), (512, 320))
+PIECES = ((0, 512), (512, 320))
 QUARTERS = ((0, 0), (0, 1), (1, 0), (1, 1))
 GROUP = tuple(sorted(range(1, 32), key=lambda k: -(2 * min(k // 8, 4 - k // 8) + min(k % 8, 8 - k % 8))))
 FAR_FIRST = (8, 7, 9, 6, 10, 5, 11, 4, 12, 3, 13, 2, 14, 1, 15)
@@ -157,31 +157,38 @@
         pl.semaphore_signal(barrier, inc=1, device_id=to_z(k), device_id_type=MESH)
 
     loads, core_copies = [], []
-    load_s = pltpu.make_async_copy(s_hbm, s_ref, w_sem.at[2])
+    load_s = pltpu.make_async_copy(s_hbm, s_ref, w_sem.at[4])
     load_s.start()
-    for half, which in enumerate((other, core)):
-        load = pltpu.make_async_copy(
-            w_hbm.at[:, pl.ds(pl.multiple_of(which * 1024, 1024), 1024)], w_ref.at[which], w_sem.at[half])
-        load.start()
-        loads.append(load)
+    halves = (other, core)
+    for half in range(2):
+        for p in range(2):
+            load = pltpu.make_async_copy(
+                w_hbm.at[:, pl.ds(pl.multiple_of(halves[half] * 1024 + p * 512, 512), 512)],
+                w_ref.at[halves[half], :, pl.ds(p * 512, 512)], w_sem.at[2 * half + p])
+            load.start()
+            loads.append(load)
 
     load_s.wait()
     st_ref[...] = s_ref[...].T
-    for half, which in enumerate((other, core)):
-        loads[half].wait()
-        for p in range(2):
-            product = jnp.dot(
-                st_ref[...], w_ref[which, :, p * 512:p * 512 + 512], preferred_element_type=jnp.float32)
-            for q in range(4):
-                part[half, p, q] = product[:, q * 128:q * 128 + 128].reshape(16, 2, 8, 128)
-            if half == 0:
-                if p == 0:
-                    pl.semaphore_wait(barrier, 46)
-                core_copies += [
-                    send(part.at[0, p, :, :, r], core_in.at[p, r], core_ss.at[p, r], core_rs.at[p, r], sibling)
-                    for r in range(2)]
+
+    def multiply(half, p):
+        loads[2 * half + p].wait()
+        product = jnp.dot(
+            st_ref[...], w_ref[halves[half], :, p * 512:p * 512 + 512], preferred_element_type=jnp.float32)
+        for q in range(4):
+            part[half, p, q] = product[:, q * 128:q * 128 + 128].reshape(16, 2, 8, 128)
+
+    for p in range(2):
+        multiply(0, p)
+        if p == 0:
+            pl.semaphore_wait(barrier, 46)
+        core_copies += [
+            send(part.at[0, p, :, :, r], core_in.at[p, r], core_ss.at[p, r], core_rs.at[p, r], sibling)
+            for r in range(2)]
     y_copies = []
     for quarter, (p, r) in enumerate(QUARTERS):
+        if r == 0:
+            multiply(1, p)
         arrive([core_copies[quarter]])
         core_sum[p, r] = part[1, p, :, :, r] + core_in[p, r]
         y_copies.append([
@@ -275,7 +282,7 @@
         product = product.reshape(4, 64, width)
         coef[:, :, first:first + width] = product
         coef_send[:, :, first:first + width] = product.astype(jnp.bfloat16)
-        lanes = pl.ds(first, width if piece < 2 else PAD - first)
+        lanes = pl.ds(first, width if piece < 1 else PAD - first)
         coef_copies.append([
             send(coef_send.at[x_of(k), :, lanes], coef_in.at[k - 1, :, lanes], c_ss.at[piece, k - 1],
                  c_rs.at[piece, k - 1], {"row": x_of(k)})
@@ -323,7 +330,7 @@
             pltpu.VMEM((4, 64, WIDTH), f32),
             pltpu.VMEM((4, 64, PAD), bf16),
             pltpu.VMEM((3, 64, PAD), bf16),
-            dma((3,)), dma((2, 2)), dma((2, 2)), dma((2, 2, 3)), dma((2, 2, 3)), dma((2, 2, 15)), dma((2, 2, 15)),
+            dma((5,)), dma((2, 2)), dma((2, 2)), dma((2, 2, 3)), dma((2, 2, 3)), dma((2, 2, 15)), dma((2, 2, 15)),
             dma((2, 2, 15)), dma((2, 2, 15)), dma((2, 3)), dma((2, 3)), dma((2,)), dma((2,)),
             dma((31,)), dma((31,)), dma((31,)), dma((31,)), dma((4, 3)), dma((4, 3)),
         ],

time: 86.3 us -> 85.5 us (level)
  no operation moved by 1% of the time
where the time goes in v5:
time: 85.5 us; the launch traced here: 85.4 us
  Pallas kernels  83.1 us (97%)
  local copies, waits for them, and re-layouts  1.66 us (2%)
    pallas_call x1, Pallas kernels, shards(): pl.pallas_call(whole, out_shape=(pltpu.VMEM((2048, R), bf16), pltpu.VMEM(...  83.1 us

profile of v5, /device:TPU:1, one launch (start us, length us, event | category | flops | bytes accessed | tf_op | source)
XLA Modules:
  0.0 85.4 jit_solution(4064197456934140140)
XLA Ops:
  0.6 83.1 %shard_map.41 = (bf16[2048,256]{1,0:T(8,128)(2,1)S(1)}, f32[64,832]{1,0:T(8,128)S(1)}) custom-call(bf16[832,2048]{1,0:T(8,128)(2,1)} %bitcast.1, bf16[832,256]{1,0:T(8,128)(2,1)} %s_hbm.1), custom_call_target="tpu_custom_call" | custom-call | tf_op jit(solution)/shard_map/pallas_call | solution.py:307
  83.7 1.0 %copy.6 = bf16[2048,256]{1,0:T(8,128)(2,1)} copy(bf16[2048,256]{1,0:T(8,128)(2,1)S(1)} %get-tuple-element.2) | data formatting | bytes 2097152
  84.7 0.7 copy.7
